TPU v7x, 256 devices: a whole 4x4x8 slice. The times are simulated.
256 devices in a mesh: seq: 16 (over z_lo, y), head: 8 (over z_hi, x), cfg: 2 (over core).
Axes of the slice: x: 4, y: 4, z: 8 (z_hi: 2, z_lo: 4; z = z_hi * 4 + z_lo), core: 2. Of those that a mesh axis runs over, the one named last changes fastest.
Arguments:
- queries: bfloat16 [12288, 5120], P(('cfg', 'seq'), 'head'), parts along dimension 0, may hold values from -16 to 16
- fresh_key: bfloat16 [12288, 5120], P(('cfg', 'seq'), 'head'), parts along dimension 0, may hold values from -16 to 16
- fresh_value: bfloat16 [12288, 5120], P(('cfg', 'seq'), 'head'), parts along dimension 0, may hold values from -6 to 6
- stale_key: bfloat16 [12288, 5120], P(('cfg', 'seq'), 'head'), parts along dimension 0, may hold values from -6 to 6
- stale_value: bfloat16 [12288, 5120], P(('cfg', 'seq'), 'head'), parts along dimension 0, may hold values from -6 to 6
- slot_tiles: int32 [96], P('cfg'), parts along dimension 0, may hold values from 0 to 47, as said below
- refresh: int32 [96], P('cfg'), parts along dimension 0, may hold values from 0 to 1, as said below
- stale_reads: int32 [32, 48], P('cfg'), parts along dimension 0, may hold values from 0 to 1, as said below
- out_weight: bfloat16 [5120, 5120], P('head'), may hold values from -6 to 6
Outputs:
- mixed: bfloat16 [12288, 5120], P(('cfg', 'seq', 'head')), parts along dimension 0
There are 2 independent parts, one for each index of `cfg`. A program takes and returns all parts, laid end to end along the dimension named above; an argument that names none is the same for every part. Nothing has to cross between parts.
Inputs may be any that keep to these rules, and one draw needn't show every extreme that they name: `slot_tiles`: A permutation of the 48 tiles. Cache slot i lies on index i // 3 of seq; the slots of every index of seq hold at least one tile that is not refreshed. `refresh`: tile t belongs to index t // 3 of seq. Every index of seq owns between 1 and 2 refreshed tiles; some index owns exactly 1 and some exactly 2. `stale_reads`: only tiles that are not refreshed are read. A reader reads at most one tile among the slots of any one index of seq; some reader reads one tile from the slots of every index.
All inputs are finite; a program needn't handle non-finite values.
Results may differ from a plain program's by a relative error of at most 0.019.
Values may be sent and summed in bfloat16 or wider, within the bound.
A program may use at most 192 MiB of HBM per device.

v0:
```python
import jax
import jax.numpy as jnp
from jax import lax
from jax.sharding import PartitionSpec as P

HD = 128
TILE = 128


NEG = -1e30


def attend(carry, query3, keys, values, mask):
    count = keys.shape[0]
    heads_here = query3.shape[1]
    keys3 = keys.reshape(count, heads_here, HD)
    values3 = values.reshape(count, heads_here, HD)
    score = jnp.einsum("qhd,khd->qhk", query3, keys3, preferred_element_type=jnp.float32) * HD ** (
        -0.5
    )
    score = jnp.where(mask[None, None, :] > 0, score, NEG)
    top_old, total_old, summed_old = carry
    top_new = jnp.maximum(top_old, jnp.max(score, axis=2))
    weight = jnp.exp(score - top_new[:, :, None]) * mask[None, None, :]
    factor = jnp.exp(top_old - top_new)
    total_new = total_old * factor + jnp.sum(weight, axis=2)
    summed_new = summed_old * factor[:, :, None] + jnp.einsum(
        "qhk,khd->qhd", weight.astype(jnp.bfloat16), values3, preferred_element_type=jnp.float32
    )
    return (top_new, total_new, summed_new)


def on_device(
    queries,
    fresh_key,
    fresh_value,
    stale_key,
    stale_value,
    slot_tiles,
    refresh,
    stale_reads,
    out_weight,
):
    tokens_here = queries.shape[0]
    heads_here = queries.shape[1] // HD
    tile_dev = tokens_here // TILE
    total_tiles = refresh.shape[0]
    readers = stale_reads.shape[0]
    width_here = queries.shape[1]
    me = lax.axis_index("seq")
    query3 = queries.reshape(tokens_here, heads_here, HD)
    tile_ids = jnp.arange(total_tiles, dtype=jnp.int32)
    empty = (
        jnp.full((tokens_here, heads_here), NEG, jnp.float32),
        jnp.zeros((tokens_here, heads_here), jnp.float32),
        jnp.zeros((tokens_here, heads_here, HD), jnp.float32),
    )
    my_reads = lax.dynamic_slice_in_dim(stale_reads, me, 1, 0)[0]
    slot_match = (slot_tiles[:, None] == tile_ids[None, :]).astype(jnp.int32)
    slot_flags = jnp.sum(slot_match * my_reads[None, :], axis=1)
    holder_valid = jnp.sum(slot_flags.reshape(readers, tile_dev), axis=1)
    stale_mask = jnp.repeat(holder_valid, TILE).astype(jnp.float32)
    my_tiles = lax.dynamic_slice_in_dim(slot_tiles, me * tile_dev, tile_dev, 0)
    own_match = (my_tiles[:, None] == tile_ids[None, :]).astype(jnp.int32)
    wanted = jnp.sum(stale_reads[:, None, :] * own_match[None, :, :], axis=2).astype(jnp.bfloat16)
    send_key = jnp.einsum(
        "sj,jrf->srf",
        wanted,
        stale_key.reshape(tile_dev, TILE, width_here),
        preferred_element_type=jnp.float32,
    ).astype(jnp.bfloat16)
    send_value = jnp.einsum(
        "sj,jrf->srf",
        wanted,
        stale_value.reshape(tile_dev, TILE, width_here),
        preferred_element_type=jnp.float32,
    ).astype(jnp.bfloat16)
    got_key, got_value = (
        lax.all_to_all(send_key, "seq", split_axis=0, concat_axis=0, tiled=True),
        lax.all_to_all(send_value, "seq", split_axis=0, concat_axis=0, tiled=True),
    )
    got_key = got_key.reshape(readers * TILE, width_here)
    got_value = got_value.reshape(readers * TILE, width_here)
    start_carry = attend(empty, query3, got_key, got_value, stale_mask)
    pieces = (
        lax.all_gather(fresh_key, "seq", axis=0, tiled=True),
        lax.all_gather(fresh_value, "seq", axis=0, tiled=True),
    )
    count = pieces[0].shape[0]
    row_tiles = jnp.arange(count, dtype=jnp.int32) // TILE
    flags = jnp.sum(
        (row_tiles[:, None] == tile_ids[None, :]).astype(jnp.int32) * refresh[None, :], axis=1
    )
    folded = attend(start_carry, query3, pieces[0], pieces[1], flags.astype(jnp.float32))
    attended = (
        (folded[2] / folded[1][:, :, None]).reshape(tokens_here, width_here).astype(jnp.bfloat16)
    )
    return lax.psum_scatter(
        jnp.dot(attended, out_weight, preferred_element_type=jnp.float32).astype(jnp.bfloat16),
        "head",
        scatter_dimension=0,
        tiled=True,
    )


def solution(mesh):
    return jax.shard_map(
        on_device,
        mesh=mesh,
        in_specs=(
            P(("cfg", "seq"), "head"),
            P(("cfg", "seq"), "head"),
            P(("cfg", "seq"), "head"),
            P(("cfg", "seq"), "head"),
            P(("cfg", "seq"), "head"),
            P("cfg"),
            P("cfg"),
            P("cfg", None),
            P("head", None),
        ),
        out_specs=P(("cfg", "seq", "head"), None),
        check_vma=False,
    )
```

profile of v0, /device:TPU:32, one launch (start us, length us, event | category | flops | bytes accessed | tf_op | source)
XLA Modules:
  0.0 545.7 jit_solution(4974885700858131936)
XLA Ops:
  6.5 2.1 copy.55
  8.6 0.7 dynamic_slice.7
  9.5 0.8 multiply_reduce_fusion
  10.3 1.4 convolution_convert_fusion.1
  11.7 2.1 copy.52
  13.8 8.7 %all-to-all-start.1 = ((bf16[16,128,640]{2,1,0:T(8,128)(2,1)}), bf16[16,128,640]{2,1,0:T(8,128)(2,1)S(1)}, u32[]{:S(2)}, u32[]{:S(2)}) async-start(bf16[16,128,640]{2,1,0:T(8,128)(2,1)} %copy.52), calls=%async_computation.1 | async-start | bytes 5242880 | tf_op jit(solution)/shard_map/all_to_all | solution.py:80
  23.2 2.0 convolution_convert_fusion.2
  25.2 2.1 copy.46
  27.3 132.7 %all-to-all-done.1 = bf16[16,128,640]{2,1,0:T(8,128)(2,1)S(1)} async-done(((bf16[16,128,640]{2,1,0:T(8,128)(2,1)}), bf16[16,128,640]{2,1,0:T(8,128)(2,1)S(1)}, u32[]{:S(2)}, u32[]{:S(2)}) %all-to-all-start.1) | async-done | bytes 2621472 | tf_op jit(solution)/shard_map/all_to_all | solution.py:80
  159.9 6.8 %all-to-all-start = ((bf16[16,128,640]{2,1,0:T(8,128)(2,1)}), bf16[16,128,640]{2,1,0:T(8,128)(2,1)}, u32[]{:S(2)}, u32[]{:S(2)}) async-start(bf16[16,128,640]{2,1,0:T(8,128)(2,1)} %copy.46), calls=%async_computation | async-start | bytes 5242880 | tf_op jit(solution)/shard_map/all_to_all | solution.py:79
  168.1 1.3 copy.48
  169.8 3.5 copy.53
  173.3 3.9 reshape_reshape.7
  177.2 125.6 %all-to-all-done = bf16[16,128,640]{2,1,0:T(8,128)(2,1)} async-done(((bf16[16,128,640]{2,1,0:T(8,128)(2,1)}), bf16[16,128,640]{2,1,0:T(8,128)(2,1)}, u32[]{:S(2)}, u32[]{:S(2)}) %all-to-all-start) | async-done | bytes 2621472 | tf_op jit(solution)/shard_map/all_to_all | solution.py:79
  302.8 7.0 %reshape.111 = bf16[2048,5,128]{2,1,0:T(8,128)(2,1)} reshape(bf16[16,128,640]{2,1,0:T(8,128)(2,1)} %all-to-all-done) | data formatting | bytes 5242880 | tf_op jit(solution)/shard_map/reshape;reshape | solution.py:16
  309.7 8.6 %bitcast_reduce_fusion.1 = (f32[384,5]{0,1:T(8,128)S(1)}, f32[5,2048,384]{2,1,0:T(8,128)}) fusion(pred[2048]{0:T(1024)(128)(4,1)S(1)} %bitcast_compare_fusion, bf16[384,5,128]{0,2,1:T(8,128)(2,1)S(1)} %bitcast.80, bf16[2048,5,128]{2,1,0:T(8,128)(2,1)} %reshape.111), kind=kOutput, calls=%fused_computation.9 | convolution fusion | flops 1018427520 | bytes 18851328 | tf_op jit(solution)/shard_map/qhd,khd->qhk/dot_general | solution.py:18
  318.4 21.1 %bitcast_reduce_fusion = (f32[384,5]{0,1:T(8,128)S(1)}, f32[5,6144,384]{2,1,0:T(8,128)}) fusion(pred[6144]{0:T(1024)(128)(4,1)S(1)} %broadcast_compare_fusion, bf16[6144,5,128]{0,2,1:T(8,128)(2,1)} %bitcast.78, bf16[384,5,128]{0,2,1:T(8,128)(2,1)S(1)} %bitcast.81), kind=kOutput, calls=%fused_computation.1 | convolution fusion | flops 3055286272 | bytes 55555584 | tf_op jit(solution)/shard_map/qhd,khd->qhk/dot_general | solution.py:18
  339.5 8.2 %fusion.8 = f32[384,5]{0,1:T(8,128)S(1)} fusion(f32[5,2048,384]{2,1,0:T(8,128)} %get-tuple-element.11, f32[2048]{0:T(1024)S(1)} %broadcast_bitcast_fusion, f32[384,5]{0,1:T(8,128)S(1)} %get-tuple-element.9, pred[2048]{0:T(1024)(128)(4,1)S(1)} %bitcast_compare_fusion), kind=kLoop, calls=%fused_computation.13 | loop fusion | flops 19658880 | bytes 15754240 | tf_op jit(solution)/shard_map/reduce_sum | solution.py:26
  347.7 22.6 %fusion.2 = f32[384,5]{0,1:T(8,128)S(1)} fusion(f32[5,6144,384]{2,1,0:T(8,128)} %get-tuple-element.13, f32[6144]{0:T(1024)S(1)} %convert_element_type.64, f32[384,5]{0,1:T(8,128)S(1)} %get-tuple-element.8, pred[6144]{0:T(1024)(128)(4,1)S(1)} %broadcast_compare_fusion), kind=kLoop, calls=%fused_computation.5 | loop fusion | flops 58980480 | bytes 47232000 | tf_op jit(solution)/shard_map/reduce_sum | solution.py:26
  370.4 5.8 %fusion.26 = f32[384,5,128]{0,2,1:T(8,128)} fusion(bf16[2048,5,128]{0,2,1:T(8,128)(2,1)S(1)} %reshape_reshape.7, f32[5,2048,384]{2,1,0:T(8,128)S(1)} %bitcast.75, f32[2048]{0:T(1024)S(1)} %broadcast_bitcast_fusion, f32[384,5]{0,1:T(8,128)S(1)} %get-tuple-element.9, pred[2048]{0:T(1024)(128)(4,1)S(1)} %bitcast_compare_fusion, ...), kind=kOutput, calls=%fused_computation.25 | convolution fusion | flops 1026785280 | bytes 19366400 | tf_op jit(solution)/shard_map/qhk,khd->qhd/dot_general | solution.py:27
  376.2 10.8 %copy.58 = bf16[6144,640]{0,1:T(8,128)(2,1)} copy(bf16[6144,640]{1,0:T(8,128)(2,1)} %all-gather.5.cloned.1.call-done) | data formatting | bytes 15728640 | tf_op jit(solution)/shard_map/all_gather | solution.py:87
  387.0 22.9 %divide_convert_fusion = bf16[384,5,128]{0,2,1:T(8,128)(2,1)S(1)} fusion(f32[384,5,128]{0,2,1:T(8,128)} %fusion.26, bf16[6144,5,128]{0,2,1:T(8,128)(2,1)} %bitcast.79, f32[5,6144,384]{2,1,0:T(8,128)} %get-tuple-element.13, f32[6144]{0:T(1024)S(1)} %convert_element_type.64, f32[384,5]{0,1:T(8,128)S(1)} %get-tuple-element.8, ...), kind=kOutput, calls=%fused_computation.28 | convolution fusion | flops 3079618560 | bytes 56570880 | tf_op jit(solution)/shard_map/qhk,khd->qhd/dot_general | solution.py:27
  409.9 4.8 convolution_convert_fusion
  414.8 124.4 %reduce-scatter.2.cloned.1.call-done = bf16[48,5120]{1,0:T(8,128)(2,1)} async-done(((bf16[384,5120]{1,0:T(8,128)(2,1)}), bf16[48,5120]{1,0:T(8,128)(2,1)}) %reduce-scatter.2.cloned.1.call-update) | async-done | bytes 491536 | tf_op jit(solution)/shard_map/reduce_scatter | solution.py:98
  (44 shorter events, 2.6 us)
Async XLA Ops:
  6.5 3.8 copy-start
  6.5 161.1 %copy-start.3 = (s32[48]{0:T(128)S(1)}, s32[48]{0:T(128)}, u32[]{:S(2)}) copy-start(s32[48]{0:T(128)} %param.14) | copy-start | bytes 580
  6.5 162.8 %copy-start.2 = (s32[48]{0:T(128)S(1)}, s32[48]{0:T(128)}, u32[]{:S(2)}) copy-start(s32[48]{0:T(128)} %param.15) | copy-start | bytes 580
  6.5 311.8 %all-gather.3.cloned.1.call-start = ((), (), s32[]{:S(2)}) async-start(), calls=%async_computation.3 | async-start | bytes 8355840 | tf_op jit(solution)/shard_map/all_gather | solution.py:86
  13.8 146.1 %all-to-all-start.1 = ((bf16[16,128,640]{2,1,0:T(8,128)(2,1)}), bf16[16,128,640]{2,1,0:T(8,128)(2,1)S(1)}, u32[]{:S(2)}, u32[]{:S(2)}) async-start(bf16[16,128,640]{2,1,0:T(8,128)(2,1)} %copy.52), calls=%async_computation.1 | async-start | bytes 5242880 | tf_op jit(solution)/shard_map/all_to_all | solution.py:80
  22.4 353.7 %all-gather.5.cloned.1.call-start = ((), (), s32[]{:S(2)}) async-start(), calls=%async_computation.4 | async-start | bytes 8355840 | tf_op jit(solution)/shard_map/all_gather | solution.py:87
  159.9 142.8 %all-to-all-start = ((bf16[16,128,640]{2,1,0:T(8,128)(2,1)}), bf16[16,128,640]{2,1,0:T(8,128)(2,1)}, u32[]{:S(2)}, u32[]{:S(2)}) async-start(bf16[16,128,640]{2,1,0:T(8,128)(2,1)} %copy.46), calls=%async_computation | async-start | bytes 5242880 | tf_op jit(solution)/shard_map/all_to_all | solution.py:79
  166.7 372.4 %reduce-scatter.2.cloned.1.call-start = ((), (), s32[]{:S(2)}) async-start(), calls=%async_computation.5 | async-start | bytes 4423680 | tf_op jit(solution)/shard_map/reduce_scatter | solution.py:98
  339.5 30.8 %slice-start = ((s8[15728640]{0:T(1024)(128)(4,1)}), s8[4194304]{0:T(1024)(128)(4,1)S(1)}, s32[]{:S(2)}) async-start(s8[15728640]{0:T(1024)(128)(4,1)} %bitcast.74), calls=%async_computation.6 | async-start | bytes 8388608
  347.7 22.7 %slice-start.1 = ((s8[15728640]{0:T(1024)(128)(4,1)}), s8[4194304]{0:T(1024)(128)(4,1)S(1)}, s32[]{:S(2)}) async-start(s8[15728640]{0:T(1024)(128)(4,1)} %bitcast.74), calls=%async_computation.7 | async-start | bytes 8388608
  347.7 22.7 %slice-start.2 = ((s8[15728640]{0:T(1024)(128)(4,1)}), s8[4194304]{0:T(1024)(128)(4,1)S(1)}, s32[]{:S(2)}) async-start(s8[15728640]{0:T(1024)(128)(4,1)} %bitcast.74), calls=%async_computation.8 | async-start | bytes 8388608
  347.7 22.7 %slice-start.3 = ((s8[15728640]{0:T(1024)(128)(4,1)}), s8[3145728]{0:T(1024)(128)(4,1)S(1)}, s32[]{:S(2)}) async-start(s8[15728640]{0:T(1024)(128)(4,1)} %bitcast.74), calls=%async_computation.9 | async-start | bytes 6291456
  376.1 33.7 %slice-start.4 = ((s8[6553600]{0:T(1024)(128)(4,1)}), s8[2359296]{0:T(1024)(128)(4,1)S(1)}, s32[]{:S(2)}) async-start(s8[6553600]{0:T(1024)(128)(4,1)} %bitcast.76), calls=%async_computation.10 | async-start | bytes 4718592
  387.0 23.0 %slice-start.5 = ((s8[6553600]{0:T(1024)(128)(4,1)}), s8[4194304]{0:T(1024)(128)(4,1)S(1)}, s32[]{:S(2)}) async-start(s8[6553600]{0:T(1024)(128)(4,1)} %bitcast.76), calls=%async_computation.11 | async-start | bytes 8388608
  387.0 152.2 %copy-start.1 = (bf16[384,640]{1,0:T(8,128)(2,1)S(1)}, bf16[384,640]{1,0:T(8,128)(2,1)}, u32[]{:S(2)}) copy-start(bf16[384,640]{1,0:T(8,128)(2,1)} %param.13) | copy-start | bytes 1474564
Sparse Core Ops, SparseCore 0:
  9.2 148.8 all-gather.2
  159.8 141.0 all-gather.4
  414.9 124.2 reduce-scatter.1
where the time goes:
time: 548 us; the launch traced here: 546 us
  waiting for transfers between devices  383 us (70%)
  matrix products  66.6 us (12%)
  local copies, waits for them, and re-layouts  34.3 us (6%)
  other arithmetic  32.3 us (6%)
  starting transfers between devices  15.7 us (3%)
  between operations  13.3 us (2%)
    all_to_all x1, waiting for transfers between devices, on_device(): lax.all_to_all(send_value, 'seq', split_axis=0, concat_axis=0, tiled=True)  133 us
    all_to_all x1, waiting for transfers between devices, on_device(): lax.all_to_all(send_key, 'seq', split_axis=0, concat_axis=0, tiled=True)  126 us
    reduce_scatter x1, waiting for transfers between devices, on_device(): lax.psum_scatter(jnp.dot(attended, out_weight, preferred_element_type=jnp...  124 us
    reduce_sum x2, other arithmetic, attend(): total_new = total_old * factor + jnp.sum(weight, axis=2)  30.7 us
    dot_general x2, matrix products, attend(): jnp.einsum('qhd,khd->qhk', query3, keys3, preferred_element_type=jnp.floa...  29.7 us
    dot_general x2, matrix products, attend(): jnp.einsum('qhk,khd->qhd', weight.astype(jnp.bfloat16), values3, preferre...  28.7 us
  transfers between devices with their start and end apart: 5, of which 3 were waited for; matrix products, arithmetic and copies ran while one was open for 17% of the time, Pallas kernels for 0%

commit v1 on v0

v1 whole, which is shorter than its diff:
```python
import functools
import math

import jax
import jax.numpy as jnp
from jax import lax
from jax.experimental import pallas as pl
from jax.experimental.pallas import tpu as pltpu
from jax.sharding import PartitionSpec as P

HD = 128
TILE = 128
SIDE = 4
MESH = pl.DeviceIdType.MESH
NEG = -1e30
LOG2_SCALE = HD ** (-0.5) * math.log2(math.e)
BF16 = jnp.bfloat16
F32 = jnp.float32


def seq_place():
    me = lax.axis_index("seq")
    return me // SIDE, lax.rem(me, SIDE)


def row_peer(zi, yi, step):
    other = lax.rem(yi + step, SIDE)
    return other, {"seq": zi * SIDE + other}


def column_peer(zi, yi, step):
    other = lax.rem(zi + step, SIDE)
    return other, {"seq": other * SIDE + yi}


def greet(devices):
    barrier = pltpu.get_barrier_semaphore()
    for device in devices:
        pl.semaphore_signal(barrier, inc=1, device_id=device, device_id_type=MESH)
    pl.semaphore_wait(barrier, len(devices))


def remote(src, dst, send_sem, recv_sem, device):
    return pltpu.make_async_remote_copy(
        src_ref=src,
        dst_ref=dst,
        send_sem=send_sem,
        recv_sem=recv_sem,
        device_id=device,
        device_id_type=MESH,
    )


def spread_kernel(
    refresh,
    q_ref,
    fk_ref,
    fv_ref,
    sk_ref,
    sv_ref,
    qall,
    kv,
    qpack,
    pack,
    send_q,
    recv_q,
    send_z,
    recv_z,
    send_kv,
    recv_kv,
):
    zi, yi = seq_place()
    me = zi * SIDE + yi
    heads = q_ref.shape[1] // HD
    last = heads - 1
    for h in range(heads):
        qpack[h] = q_ref[:, h * HD : (h + 1) * HD]
    rows = [row_peer(zi, yi, step) for step in (2, 1, 3)]
    columns = [column_peer(zi, yi, step) for step in (1, 2, 3)]
    greet([device for _, device in rows + columns])
    copies = []
    first = []
    for slot, (other, device) in enumerate(rows):
        copy = remote(
            qpack.at[other], qall.at[zi, yi], send_q.at[slot], recv_q.at[slot], device
        )
        copy.start()
        first.append(copy)
    qall[zi, yi] = qpack[yi]
    qall[zi, last] = qpack[last]

    r0 = refresh[3 * me]
    r1 = refresh[3 * me + 1]
    r2 = refresh[3 * me + 2]
    one = jnp.where(r0 > 0, 0, jnp.where(r1 > 0, 1, 2))
    two = jnp.where(r2 > 0, 2, 1)

    def fill(h):
        cut = slice(h * HD, (h + 1) * HD)
        for kind, (fresh, stale) in enumerate(((fk_ref, sk_ref), (fv_ref, sv_ref))):
            pack[h, kind, 0:TILE] = fresh[one, :, cut]
            pack[h, kind, TILE : 2 * TILE] = fresh[two, :, cut]
            for tile in range(3):
                pack[h, kind, (2 + tile) * TILE : (3 + tile) * TILE] = stale[tile, :, cut]

    for h in range(heads):
        fill(h)
    for slot, (other, device) in enumerate(rows):
        for part, source in enumerate((other, last)):
            copy = remote(
                pack.at[source],
                kv.at[yi, pl.ds(2 * part, 2)],
                send_kv.at[slot, part],
                recv_kv.at[slot, part],
                device,
            )
            copy.start()
            copies.append(copy)
    kv[yi, 0:2] = pack[yi]
    kv[yi, 2:4] = pack[last]
    for copy in first:
        copy.wait_recv()
    for slot, (other, device) in enumerate(columns):
        copy = remote(qall.at[zi], qall.at[zi], send_z.at[slot], recv_z.at[slot], device)
        copy.start()
        copies.append(copy)
    for copy in first:
        copy.wait_send()
    for copy in copies:
        copy.wait()


def spread(refresh, queries, fresh_key, fresh_value, stale_key, stale_value):
    tokens, width = queries.shape
    heads = width // HD
    tiles = [x.reshape(3, TILE, width) for x in (fresh_key, fresh_value, stale_key, stale_value)]
    vmem = pl.BlockSpec(memory_space=pltpu.VMEM)
    return pl.pallas_call(
        spread_kernel,
        out_shape=(
            jax.ShapeDtypeStruct((SIDE, heads, tokens, HD), BF16),
            jax.ShapeDtypeStruct((SIDE, 4, 5 * TILE, HD), BF16),
        ),
        in_specs=[pl.BlockSpec(memory_space=pltpu.SMEM)] + [vmem] * 5,
        out_specs=(vmem, vmem),
        scratch_shapes=[
            pltpu.VMEM((heads, tokens, HD), BF16),
            pltpu.VMEM((heads, 2, 5 * TILE, HD), BF16),
            pltpu.SemaphoreType.DMA((3,)),
            pltpu.SemaphoreType.DMA((3,)),
            pltpu.SemaphoreType.DMA((3,)),
            pltpu.SemaphoreType.DMA((3,)),
            pltpu.SemaphoreType.DMA((3, 2)),
            pltpu.SemaphoreType.DMA((3, 2)),
        ],
        compiler_params=pltpu.CompilerParams(
            collective_id=0, has_side_effects=True, vmem_limit_bytes=48 * 2**20
        ),
        name="spread",
    )(refresh, queries, *tiles)


def attend_kernel(heads, refresh, slots, reads, q_ref, kv, o_ref, lse_ref, keys, values, bias, stats):
    zi, yi = seq_place()
    item = pl.program_id(0)
    zr = item // heads
    place = lax.rem(item, heads)
    is_last = place == heads - 1
    reader = zr * SIDE + jnp.where(is_last, yi, place)
    bank = jnp.where(is_last, 1, 0)
    fresh_rows = SIDE * 2 * TILE

    @pl.when(item == 0)
    def _():
        for part in range(2):
            for source in range(SIDE):
                cut = slice(source * 2 * TILE, (source + 1) * 2 * TILE)
                keys[part, cut] = kv[source, 2 * part, 0 : 2 * TILE]
                values[part, cut] = kv[source, 2 * part + 1, 0 : 2 * TILE]
        for source in range(SIDE):
            base = 3 * (zi * SIDE + source)
            count = refresh[base] + refresh[base + 1] + refresh[base + 2]
            cut = source * 2 * TILE
            bias[0:1, cut : cut + TILE] = jnp.zeros((1, TILE), F32)
            bias[0:1, cut + TILE : cut + 2 * TILE] = jnp.full(
                (1, TILE), jnp.where(count > 1, 0.0, NEG), F32
            )

    for source in range(SIDE):
        base = 3 * (zi * SIDE + source)
        flags = [reads[reader, slots[base + j]] for j in range(3)]
        pick = jnp.where(flags[1] > 0, 1, jnp.where(flags[2] > 0, 2, 0))
        start = pl.multiple_of((2 + pick) * TILE, TILE)
        cut = slice(fresh_rows + source * TILE, fresh_rows + (source + 1) * TILE)
        keys[bank, cut] = kv[source, 2 * bank, pl.ds(start, TILE)]
        values[bank, cut] = kv[source, 2 * bank + 1, pl.ds(start, TILE)]
        used = flags[0] + flags[1] + flags[2]
        bias[0:1, cut] = jnp.full((1, TILE), jnp.where(used > 0, 0.0, NEG), F32)

    k = keys[bank]
    v = values[bank]
    b = bias[0:1, :]
    tokens = q_ref.shape[2]
    lane = lax.broadcasted_iota(jnp.int32, (TILE, HD), 1)
    for part in range(tokens // TILE):
        cut = slice(part * TILE, (part + 1) * TILE)
        score = lax.dot_general(
            q_ref[0, 0, cut], k, (((1,), (1,)), ((), ())), preferred_element_type=F32
        )
        score = score * LOG2_SCALE + b
        top = jnp.max(score, axis=1, keepdims=True)
        weight = jnp.exp2(score - top)
        total = jnp.sum(weight, axis=1, keepdims=True)
        out = lax.dot_general(
            weight.astype(BF16), v, (((1,), (0,)), ((), ())), preferred_element_type=F32
        )
        o_ref[0, 0, cut] = (out / total).astype(BF16)
        stats[cut] = jnp.where(lane == place, top + jnp.log2(total), stats[cut])

    @pl.when(is_last)
    def _():
        lse_ref[0] = stats[...].T[0:8, :]


def attend(refresh, slots, reads, qall, kv):
    side, heads, tokens, _ = qall.shape
    keys = SIDE * 3 * TILE
    spec = pl.BlockSpec((1, 1, tokens, HD), lambda i, *_: (i // heads, lax.rem(i, heads), 0, 0))
    return pl.pallas_call(
        functools.partial(attend_kernel, heads),
        out_shape=(
            jax.ShapeDtypeStruct((side, heads, tokens, HD), BF16),
            jax.ShapeDtypeStruct((side, 8, tokens), F32),
        ),
        grid_spec=pltpu.PrefetchScalarGridSpec(
            num_scalar_prefetch=3,
            grid=(side * heads,),
            in_specs=[spec, pl.BlockSpec(kv.shape, lambda i, *_: (0, 0, 0, 0))],
            out_specs=(spec, pl.BlockSpec((1, 8, tokens), lambda i, *_: (i // heads, 0, 0))),
            scratch_shapes=[
                pltpu.VMEM((2, keys, HD), BF16),
                pltpu.VMEM((2, keys, HD), BF16),
                pltpu.VMEM((8, keys), F32),
                pltpu.VMEM((tokens, HD), F32),
            ],
        ),
        compiler_params=pltpu.CompilerParams(vmem_limit_bytes=48 * 2**20),
        name="attend",
    )(refresh, slots, reads, qall, kv)


def project_kernel(
    o_ref,
    lse_ref,
    w_hbm,
    out_ref,
    w,
    orecv,
    lrecv,
    comb,
    att5,
    att,
    pbuf,
    rbuf,
    fbuf,
    own,
    zsend,
    zrecv,
    w_sem,
    send_o,
    recv_o,
    send_l,
    recv_l,
    send_a,
    recv_a,
    send_far,
    recv_far,
    send_near,
    recv_near,
    send_relay,
    recv_relay,
    send_hi,
    recv_hi,
):
    zi, yi = seq_place()
    head = lax.axis_index("head")
    zh, xi = head // SIDE, lax.rem(head, SIDE)
    right = lax.rem(xi + 1, SIDE)
    left = lax.rem(xi + SIDE - 1, SIDE)
    opposite = lax.rem(xi + 2, SIDE)
    to_right = {"head": zh * SIDE + right}
    to_left = {"head": zh * SIDE + left}
    to_hi = {"head": (1 - zh) * SIDE + xi}
    rows = [row_peer(zi, yi, step) for step in (2, 1, 3)]
    columns = [column_peer(zi, yi, step) for step in (1, 2, 3)]
    heads, tokens = o_ref.shape[1], o_ref.shape[2]
    blocks = pbuf.shape[0]
    part_rows, part_columns = pbuf.shape[3], pbuf.shape[4]

    w_copy = pltpu.make_async_copy(w_hbm, w, w_sem)
    w_copy.start()
    greet([device for _, device in rows + columns] + [to_right, to_left, to_hi])
    copies = []
    for slot, (other, device) in enumerate(columns):
        for src, dst, send, recv in (
            (lse_ref, lrecv, send_l, recv_l),
            (o_ref, orecv, send_o, recv_o),
        ):
            copy = remote(src.at[other], dst.at[zi], send.at[slot], recv.at[slot], device)
            copy.start()
            copies.append(copy)
    orecv[zi] = o_ref[zi]
    lrecv[zi] = lse_ref[zi]
    for copy in copies:
        copy.wait()

    logs = [lrecv[z] for z in range(SIDE)]
    top = functools.reduce(jnp.maximum, logs)
    shares = [jnp.exp2(x - top) for x in logs]
    total = functools.reduce(jnp.add, shares)
    shares = [x / total for x in shares]
    pad = jnp.zeros((HD - 8 * SIDE, tokens), F32)
    factors = jnp.concatenate(shares + [pad], axis=0).T
    for k in range(heads):
        mixed = jnp.zeros((tokens, HD), F32)
        for z in range(SIDE):
            mixed += orecv[z, k].astype(F32) * factors[:, z * 8 + k : z * 8 + k + 1]
        comb[k] = mixed.astype(BF16)
    copies = []
    for slot, (other, device) in enumerate(rows):
        copy = remote(comb.at[other], att5.at[yi], send_a.at[slot], recv_a.at[slot], device)
        copy.start()
        copies.append(copy)
    att5[yi] = comb[yi]
    att5[heads - 1] = comb[heads - 1]
    for copy in copies:
        copy.wait()
    for h in range(heads):
        att[:, h * HD : (h + 1) * HD] = att5[h]
    w_copy.wait()

    def plan(block):
        forward = block < blocks // 2
        ahead, behind = (right, left) if forward else (left, right)
        to_ahead, to_behind = (to_right, to_left) if forward else (to_left, to_right)
        side = 0 if forward else 1
        far = remote(
            pbuf.at[block, opposite], rbuf.at[block], send_far.at[block], recv_far.at[block], to_ahead
        )
        near = remote(
            pbuf.at[block, behind],
            fbuf.at[1 - side, block],
            send_near.at[block],
            recv_near.at[block],
            to_behind,
        )
        relay = remote(
            pbuf.at[block, ahead],
            fbuf.at[side, block],
            send_relay.at[block],
            recv_relay.at[block],
            to_ahead,
        )
        hi = remote(zsend.at[block], zrecv.at[block], send_hi.at[block], recv_hi.at[block], to_hi)
        return ahead, far, near, relay, hi

    plans = [plan(block) for block in range(blocks)]
    order = [0, blocks // 2, 1, blocks // 2 + 1]
    for block in order:
        product = jnp.dot(
            att[...],
            w[:, block * part_columns : (block + 1) * part_columns],
            preferred_element_type=F32,
        ).astype(BF16)
        for g in range(2 * SIDE):
            pbuf[block, g % SIDE, g // SIDE] = product[g * part_rows : (g + 1) * part_rows]
        _, far, near, _, _ = plans[block]
        far.start()
        near.start()
    for block in order:
        ahead, far, _, relay, _ = plans[block]
        far.wait_recv()
        pbuf[block, ahead] = (
            pbuf[block, ahead].astype(F32) + rbuf[block].astype(F32)
        ).astype(BF16)
        relay.start()
    for block in order:
        _, _, near, relay, hi = plans[block]
        near.wait_recv()
        relay.wait_recv()
        for side in range(2):
            own[block, side] = (
                pbuf[block, xi, side].astype(F32)
                + fbuf[0, block, side].astype(F32)
                + fbuf[1, block, side].astype(F32)
            )
        zsend[block] = own[block, 1 - zh].astype(BF16)
        hi.start()
    for block in order:
        hi = plans[block][4]
        hi.wait_recv()
        out_ref[:, block * part_columns : (block + 1) * part_columns] = (
            own[block, zh] + zrecv[block].astype(F32)
        ).astype(BF16)
    for block in order:
        _, far, near, relay, hi = plans[block]
        far.wait_send()
        near.wait_send()
        relay.wait_send()
        hi.wait_send()


def project(o, lse, out_weight):
    side, heads, tokens, _ = o.shape
    depth, width = out_weight.shape
    blocks = 4
    cols = width // blocks
    rows = tokens // (2 * SIDE)
    vmem = pl.BlockSpec(memory_space=pltpu.VMEM)
    dma = pltpu.SemaphoreType.DMA
    return pl.pallas_call(
        project_kernel,
        out_shape=jax.ShapeDtypeStruct((rows, width), BF16),
        in_specs=[vmem, vmem, pl.BlockSpec(memory_space=pl.ANY)],
        out_specs=vmem,
        scratch_shapes=[
            pltpu.VMEM((depth, width), BF16),
            pltpu.VMEM((side, heads, tokens, HD), BF16),
            pltpu.VMEM((side, 8, tokens), F32),
            pltpu.VMEM((heads, tokens, HD), BF16),
            pltpu.VMEM((heads, tokens, HD), BF16),
            pltpu.VMEM((tokens, depth), BF16),
            pltpu.VMEM((blocks, SIDE, 2, rows, cols), BF16),
            pltpu.VMEM((blocks, 2, rows, cols), BF16),
            pltpu.VMEM((2, blocks, 2, rows, cols), BF16),
            pltpu.VMEM((blocks, 2, rows, cols), F32),
            pltpu.VMEM((blocks, rows, cols), BF16),
            pltpu.VMEM((blocks, rows, cols), BF16),
            dma,
        ]
        + [dma((3,))] * 6
        + [dma((blocks,))] * 8,
        compiler_params=pltpu.CompilerParams(
            collective_id=1, has_side_effects=True, vmem_limit_bytes=48 * 2**20
        ),
        name="project",
    )(o, lse, out_weight)


def on_device(
    queries,
    fresh_key,
    fresh_value,
    stale_key,
    stale_value,
    slot_tiles,
    refresh,
    stale_reads,
    out_weight,
):
    qall, kv = spread(refresh, queries, fresh_key, fresh_value, stale_key, stale_value)
    o, lse = attend(refresh, slot_tiles, stale_reads, qall, kv)
    return project(o, lse, out_weight)


def solution(mesh):
    return jax.shard_map(
        on_device,
        mesh=mesh,
        in_specs=(
            P(("cfg", "seq"), "head"),
            P(("cfg", "seq"), "head"),
            P(("cfg", "seq"), "head"),
            P(("cfg", "seq"), "head"),
            P(("cfg", "seq"), "head"),
            P("cfg"),
            P("cfg"),
            P("cfg", None),
            P("head", None),
        ),
        out_specs=P(("cfg", "seq", "head"), None),
        check_vma=False,
    )
```

time: 548 us -> 207 us (0.38)
  waiting for transfers between devices: 383 us -> 0 us
  Pallas kernels: 0 us -> 199 us
  matrix products: 66.6 us -> 0 us
  other arithmetic: 32.3 us -> 0 us
  local copies, waits for them, and re-layouts: 34.3 us -> 7.93 us
  starting transfers between devices: 15.7 us -> 0 us
  between operations: 13.3 us -> 0.03 us
    all_to_all x2 -> x0, waiting for transfers between devices: 258 us -> none  [the longest x1 133 us: on_device(): lax.all_to_all(send_value, 'seq', split_axis=0, concat_axis=0, tiled=True)]
    pallas_call x0 -> x3, Pallas kernels: none -> 199 us  [the longest x1 109 us: project(): pl.pallas_call(project_kernel, out_shape=jax.ShapeDtypeStruct((rows, widt...]
    reduce_scatter x1 -> x0, waiting for transfers between devices: 124 us -> none  [on_device(): lax.psum_scatter(jnp.dot(attended, out_weight, preferred_element_type=jnp...]
    dot_general x7 -> x0, matrix products: 66.6 us -> none  [the longest x2 29.7 us: attend(): jnp.einsum('qhd,khd->qhk', query3, keys3, preferred_element_type=jnp.floa...]
    reduce_sum x6 -> x0, other arithmetic: 32.1 us -> none  [the longest x2 30.7 us: attend(): total_new = total_old * factor + jnp.sum(weight, axis=2)]
    all_to_all x2 -> x0, starting transfers between devices: 15.4 us -> none  [the longest x1 8.65 us: on_device(): lax.all_to_all(send_value, 'seq', split_axis=0, concat_axis=0, tiled=True)]
    another operation x2 -> x0, local copies, waits for them, and re-layouts: 10.9 us -> none  [the longest x1 6.98 us: attend(): keys3 = keys.reshape(count, heads_here, HD)]
    all_gather x1 -> x0, local copies, waits for them, and re-layouts: 10.8 us -> none  [on_device(): lax.all_gather(fresh_value, 'seq', axis=0, tiled=True)]
  transfers between devices with their start and end apart: 5 -> 0, of which waited for: 3 -> 0; matrix products, arithmetic and copies ran while one was open for 17% -> 0% of each run, Pallas kernels for 0% -> 0%
where the time goes in v1:
time: 207 us
  Pallas kernels  199 us (96%)
  local copies, waits for them, and re-layouts  7.93 us (4%)
    pallas_call x1, Pallas kernels, project(): pl.pallas_call(project_kernel, out_shape=jax.ShapeDtypeStruct((rows, widt...  109 us
    pallas_call x1, Pallas kernels, spread(): pl.pallas_call(spread_kernel, out_shape=(jax.ShapeDtypeStruct((SIDE, head...  57.3 us
    pallas_call x1, Pallas kernels, attend(): pl.pallas_call(functools.partial(attend_kernel, heads), out_shape=(jax.Sh...  32.8 us
    unnamed x17, local copies, waits for them, and re-layouts  7.93 us

profile of v1, /device:TPU:32, one launch (start us, length us, event | category | flops | bytes accessed | tf_op | source)
XLA Modules:
  0.0 206.8 jit_solution(8101199929502410251)
XLA Ops:
  0.0 0.0 copy-start
  0.0 1.0 copy-done
  1.0 0.0 copy-start.1
  1.0 1.0 copy-done.1
  2.1 0.0 copy-start.2
  2.1 1.0 copy-done.2
  3.1 0.0 copy-start.3
  3.1 1.0 copy-done.3
  4.1 0.0 copy-start.4
  4.1 1.0 copy-done.4
  5.2 0.0 copy-start.6
  5.2 0.7 copy-done.6
  5.8 57.3 %spread.1 = (bf16[4,5,384,128]{3,2,1,0:T(8,128)(2,1)S(1)}, bf16[4,4,640,128]{3,2,1,0:T(8,128)(2,1)}) custom-call(s32[48]{0:T(128)S(1)} %copy-done.6, bf16[384,640]{1,0:T(8,128)(2,1)S(1)} %copy-done, bf16[3,128,640]{2,1,0:T(8,128)(2,1)S(1)} %bitcast.4, bf16[3,128,640]{2,1,0:T(8,128)(2,1)S(1)} %bitcast.5, bf16[3,128,640]{2,1,0:T(8,128)(2,1)S(1)} %bitcast.6, ...), custom_call_target="tpu_custom_call" | custom-call | tf_op jit(solution)/shard_map/spread/pallas_call | solution.py:138
  63.2 0.0 copy-start.5
  63.2 0.7 copy-done.5
  63.9 0.0 copy-start.7
  63.9 0.7 copy-done.7
  64.5 32.8 %attend.1 = (bf16[4,5,384,128]{3,2,1,0:T(8,128)(2,1)S(1)}, f32[4,8,384]{2,1,0:T(8,128)S(1)}) custom-call(s32[48]{0:T(128)S(1)} %copy-done.6, s32[48]{0:T(128)S(1)} %copy-done.7, s32[16,48]{1,0:T(8,128)S(1)} %copy-done.5, bf16[4,5,384,128]{3,2,1,0:T(8,128)(2,1)S(1)} %get-tuple-element.9.q_ref, bf16[4,4,640,128]{3,2,1,0:T(8,128)(2,1)} %get-tuple-element.10.kv), custom_call_target="tpu_custom_call" | custom-call | tf_op jit(solution)/shard_map/attend/pallas_call | solution.py:229
  97.3 108.7 %project.1 = bf16[48,5120]{1,0:T(8,128)(2,1)S(1)} custom-call(bf16[4,5,384,128]{3,2,1,0:T(8,128)(2,1)S(1)} %get-tuple-element.11.o_ref, f32[4,8,384]{2,1,0:T(8,128)S(1)} %get-tuple-element.12.lse_ref, bf16[640,5120]{1,0:T(8,128)(2,1)} %w_hbm.1), custom_call_target="tpu_custom_call" | custom-call | tf_op jit(solution)/shard_map/project/pallas_call | solution.py:421
  206.0 0.8 copy.11
Async XLA Ops:
  0.0 1.0 copy-start
  1.0 1.0 copy-start.1
  2.1 1.0 copy-start.2
  3.1 1.0 copy-start.3
  4.1 1.0 copy-start.4
  5.2 0.7 copy-start.6
  63.2 0.7 copy-start.5
  63.9 0.7 copy-start.7

commit v2 on v0

v2 whole, which is shorter than its diff:
```python
import functools
import math

import jax
import jax.numpy as jnp
from jax import lax
from jax.experimental import pallas as pl
from jax.experimental.pallas import tpu as pltpu
from jax.sharding import PartitionSpec as P

HD = 128
TILE = 128
SIDE = 4
HEADS = 5
SLOTS = 5
HALVES = 2
BLOCKS = 4
LANES = 256
MESH = pl.DeviceIdType.MESH
NEG = -1e30
LOG2_SCALE = HD ** (-0.5) * math.log2(math.e)
BF16 = jnp.bfloat16
F32 = jnp.float32


def kernel(
    refresh,
    wanted,
    q_hbm,
    fk_hbm,
    fv_hbm,
    sk_hbm,
    sv_hbm,
    w_hbm,
    out_ref,
    qpack,
    fresh,
    pack,
    qall,
    kv,
    keys,
    values,
    bias,
    stats,
    o_own,
    l_own,
    o_near,
    l_near,
    o_far,
    l_far,
    o_merge,
    l_merge,
    comb,
    att5,
    w,
    pbuf,
    rbuf,
    fbuf,
    zsend,
    zrecv,
    local_sem,
    send_sem,
    recv_sem,
):
    me = lax.axis_index("seq")
    head = lax.axis_index("head")
    zi, yi = me // SIDE, lax.rem(me, SIDE)
    zh, xi = head // SIDE, lax.rem(head, SIDE)
    right = lax.rem(xi + 1, SIDE)
    left = lax.rem(xi + SIDE - 1, SIDE)
    opposite = lax.rem(xi + 2, SIDE)
    to_right = {"head": zh * SIDE + right}
    to_left = {"head": zh * SIDE + left}
    to_hi = {"head": (1 - zh) * SIDE + xi}
    z1 = zi + 1 - 2 * lax.rem(zi, 2)
    z2 = lax.rem(zi + 2, SIDE)
    z3 = SIDE - 1 - zi
    to_z1 = {"seq": z1 * SIDE + yi}
    to_z2 = {"seq": z2 * SIDE + yi}
    row = []
    for step in (2, 1, 3):
        other = lax.rem(yi + step, SIDE)
        row.append((other, {"seq": zi * SIDE + other}))
    last = HEADS - 1
    tokens = qpack.shape[1]
    half = tokens // HALVES
    started = []
    count = [0]

    def remote(src, dst, device):
        index = count[0]
        count[0] += 1
        copy = pltpu.make_async_remote_copy(
            src_ref=src,
            dst_ref=dst,
            send_sem=send_sem.at[index],
            recv_sem=recv_sem.at[index],
            device_id=device,
            device_id_type=MESH,
        )
        started.append(copy)
        return copy

    def send(src, dst, device):
        copy = remote(src, dst, device)
        copy.start()
        return copy

    local_count = [0]

    def load(src, dst):
        copy = pltpu.make_async_copy(src, dst, local_sem.at[local_count[0]])
        local_count[0] += 1
        copy.start()
        return copy

    def lanes(h):
        return pl.ds(h * HD, HD)

    q_loads = [load(q_hbm.at[:, lanes(h)], qpack.at[h]) for h in range(HEADS)]
    fresh_loads = [load(x, fresh.at[i]) for i, x in enumerate((fk_hbm, fv_hbm))]
    stale_loads = []
    for h in range(HEADS):
        for kind, x in enumerate((sk_hbm, sv_hbm)):
            stale_loads.append(
                load(x.at[:, lanes(h)], pack.at[h, kind, pl.ds(2 * TILE, 3 * TILE)])
            )

    barrier = pltpu.get_barrier_semaphore()
    peers = [device for _, device in row] + [to_z1, to_z2, to_right, to_left, to_hi]
    for device in peers:
        pl.semaphore_signal(barrier, inc=1, device_id=device, device_id_type=MESH)
    pl.semaphore_wait(barrier, len(peers))

    for copy in q_loads:
        copy.wait()
    row_q = [send(qpack.at[other], qall.at[zi, yi], device) for other, device in row]
    qall[zi, yi] = qpack[yi]
    qall[zi, last] = qpack[last]

    r0 = refresh[3 * me]
    r1 = refresh[3 * me + 1]
    r2 = refresh[3 * me + 2]
    for copy in fresh_loads:
        copy.wait()
    for h in range(HEADS):
        for kind in range(2):
            tile0, tile1, tile2 = [fresh[kind, i, :, h * HD : (h + 1) * HD] for i in range(3)]
            pack[h, kind, 0:TILE] = jnp.where(r0 > 0, tile0, jnp.where(r1 > 0, tile1, tile2))
            pack[h, kind, TILE : 2 * TILE] = jnp.where(r2 > 0, tile2, tile1)
    for copy in stale_loads:
        copy.wait()
    row_kv = []
    for other, device in row:
        for part, source in enumerate((other, last)):
            row_kv.append(send(pack.at[source], kv.at[yi, pl.ds(2 * part, 2)], device))
    w_load = load(w_hbm, w)
    kv[yi, 0:2] = pack[yi]
    kv[yi, 2:4] = pack[last]
    values[:, :, HD:] = jnp.ones((2, values.shape[1], HD), BF16)
    stats[...] = jnp.zeros(stats.shape, F32)

    for copy in row_q:
        copy.wait_recv()
    q_far = send(qall.at[zi], qall.at[zi], to_z2)
    q_near = send(qall.at[zi], qall.at[zi], to_z1)
    q_far.wait_recv()
    q_relay = send(qall.at[z2], qall.at[z2], to_z1)

    for copy in row_kv:
        copy.wait_recv()
    for part in range(2):
        for source in range(SIDE):
            cut = slice(source * 2 * TILE, (source + 1) * 2 * TILE)
            keys[part, cut] = kv[source, 2 * part, 0 : 2 * TILE]
            values[part, cut, 0:HD] = kv[source, 2 * part + 1, 0 : 2 * TILE]
    for source in range(SIDE):
        base = 3 * (zi * SIDE + source)
        filled = refresh[base] + refresh[base + 1] + refresh[base + 2]
        cut = source * 2 * TILE
        bias[0:1, cut : cut + TILE] = jnp.zeros((1, TILE), F32)
        bias[0:1, cut + TILE : cut + 2 * TILE] = jnp.full(
            (1, TILE), jnp.where(filled > 1, 0.0, NEG), F32
        )

    fresh_rows = SIDE * 2 * TILE

    def attend(t, zr, place):
        start_row = pl.multiple_of(jnp.where(t == 0, 1 - zh, zh) * half, half)

        def item(k, carry):
            is_last = jnp.where(k == last, 1, 0)
            reader = zr * SIDE + k * (1 - is_last) + yi * is_last
            for source in range(SIDE):
                base = 3 * (zi * SIDE + source)
                flags = [wanted[reader, base + j] for j in range(3)]
                cut = slice(fresh_rows + source * TILE, fresh_rows + (source + 1) * TILE)

                def pick(kind):
                    tile0, tile1, tile2 = [
                        kv[source, kind, (2 + j) * TILE : (3 + j) * TILE] for j in range(3)
                    ]
                    return jnp.where(flags[1] > 0, tile1, jnp.where(flags[2] > 0, tile2, tile0))

                keys[is_last, cut] = pick(2 * is_last)
                values[is_last, cut, 0:HD] = pick(2 * is_last + 1)
                used = flags[0] + flags[1] + flags[2]
                bias[0:1, cut] = jnp.full((1, TILE), jnp.where(used > 0, 0.0, NEG), F32)
            score = lax.dot_general(
                qall[zr, k, pl.ds(start_row, half)],
                keys[is_last],
                (((1,), (1,)), ((), ())),
                preferred_element_type=F32,
            )
            score = score * LOG2_SCALE + bias[0:1, :]
            top = jnp.max(score, axis=1, keepdims=True)
            weight = jnp.exp2(score - top).astype(BF16)
            both = jnp.dot(weight, values[is_last], preferred_element_type=F32)
            total = both[:, HD:]
            o_own[t, place, k] = (both[:, :HD] / total).astype(BF16)
            lane = lax.broadcasted_iota(jnp.int32, (half, HD), 1)
            stats[0:half] = jnp.where(lane == k, top + jnp.log2(total), stats[0:half])
            return carry

        lax.fori_loop(0, HEADS, item, 0)
        l_own[t, place] = stats[...].T[0:8, :]

    def shares(logs):
        top = functools.reduce(jnp.maximum, logs)
        parts = [jnp.exp2(x - top) for x in logs]
        total = functools.reduce(jnp.add, parts)
        parts = [x / total for x in parts]
        pad = jnp.zeros((HD - 8 * len(logs), LANES), F32)
        return top + jnp.log2(total), jnp.concatenate(parts + [pad], axis=0).T

    def mix(pieces, factors, k):
        mixed = jnp.zeros((half, HD), F32)
        for i, piece in enumerate(pieces):
            mixed += piece.astype(F32) * factors[0:half, 8 * i + k : 8 * i + k + 1]
        return mixed.astype(BF16)

    near_copies = [[], []]
    far_copies = [[], []]
    row_copies = [[], []]

    def return_near(t, place, slot):
        near_copies[t].append(send(o_own.at[t, place], o_near.at[t, slot], to_z1))
        near_copies[t].append(send(l_own.at[t, place], l_near.at[t, slot], to_z1))

    def merge(t):
        for copy in near_copies[t]:
            copy.wait_recv()
        l_merge[t], factors = shares([l_own[t, 2], l_near[t, 1]])
        for k in range(HEADS):
            o_merge[t, k] = mix([o_own[t, 2, k], o_near[t, 1, k]], factors, k)
        far_copies[t].append(send(o_merge.at[t], o_far.at[t], to_z2))
        far_copies[t].append(send(l_merge.at[t], l_far.at[t], to_z2))

    def combine(t):
        for copy in far_copies[t]:
            copy.wait_recv()
        _, factors = shares([l_own[t, 0], l_near[t, 0], l_far[t]])
        for k in range(HEADS):
            comb[t, k] = mix([o_own[t, 0, k], o_near[t, 0, k], o_far[t, k]], factors, k)
        for other, device in row:
            row_copies[t].append(send(comb.at[t, other], att5.at[t, yi], device))
        att5[t, yi] = comb[t, yi]
        att5[t, last] = comb[t, last]

    part_rows, part_columns = pbuf.shape[3], pbuf.shape[4]
    order = (0, BLOCKS // 2, 1, BLOCKS // 2 + 1)
    plans = {}
    for t in range(HALVES):
        for block in order:
            forward = block < BLOCKS // 2
            ahead, behind = (right, left) if forward else (left, right)
            to_ahead, to_behind = (to_right, to_left) if forward else (to_left, to_right)
            side = 0 if forward else 1
            plans[t, block] = (
                ahead,
                remote(pbuf.at[t, block, opposite], rbuf.at[t, block], to_ahead),
                remote(pbuf.at[t, block, behind], fbuf.at[1 - side, t, block], to_behind),
                remote(pbuf.at[t, block, ahead], fbuf.at[side, t, block], to_ahead),
            )
    hi_plans = {block: remote(zsend.at[block], zrecv.at[block], to_hi) for block in order}

    def project(t):
        for copy in row_copies[t]:
            copy.wait_recv()
        att = jnp.concatenate([att5[t, h] for h in range(HEADS)], axis=1)
        for block in order:
            product = jnp.dot(
                att,
                w[:, block * part_columns : (block + 1) * part_columns],
                preferred_element_type=F32,
            ).astype(BF16)
            for x in range(SIDE):
                pbuf[t, block, x] = product[x * part_rows : (x + 1) * part_rows]
            _, far, near, _ = plans[t, block]
            far.start()
            near.start()

    def relay(t):
        for block in order:
            ahead, far, _, onward = plans[t, block]
            far.wait_recv()
            pbuf[t, block, ahead] = (
                pbuf[t, block, ahead].astype(F32) + rbuf[t, block].astype(F32)
            ).astype(BF16)
            onward.start()

    def reduced(t, block):
        _, _, near, onward = plans[t, block]
        near.wait_recv()
        onward.wait_recv()
        return (
            pbuf[t, block, xi].astype(F32)
            + fbuf[0, t, block].astype(F32)
            + fbuf[1, t, block].astype(F32)
        )

    attend(0, zi, 0)
    q_near.wait_recv()
    attend(0, z1, 1)
    return_near(0, 1, 0)
    q_relay.wait_recv()
    attend(0, z3, 3)
    return_near(0, 3, 1)
    attend(0, z2, 2)
    attend(1, z1, 1)
    return_near(1, 1, 0)
    merge(0)
    attend(1, z3, 3)
    return_near(1, 3, 1)
    attend(1, z2, 2)
    combine(0)
    attend(1, zi, 0)
    merge(1)
    w_load.wait()
    project(0)
    relay(0)
    combine(1)
    for block in order:
        zsend[block] = reduced(0, block).astype(BF16)
        hi_plans[block].start()
    project(1)
    relay(1)
    for block in order:
        total = reduced(1, block)
        hi_plans[block].wait_recv()
        out_ref[:, block * part_columns : (block + 1) * part_columns] = (
            total + zrecv[block].astype(F32)
        ).astype(BF16)
    for copy in started:
        copy.wait_send()


def on_device(
    queries,
    fresh_key,
    fresh_value,
    stale_key,
    stale_value,
    slot_tiles,
    refresh,
    stale_reads,
    out_weight,
):
    tokens, width = queries.shape
    depth, columns = out_weight.shape
    half = tokens // HALVES
    rows = half // SIDE
    cols = columns // BLOCKS
    keys = SIDE * 3 * TILE
    tiles = jnp.arange(refresh.shape[0], dtype=jnp.int32)
    held = (slot_tiles[:, None] == tiles[None, :]).astype(jnp.int32)
    wanted = jnp.sum(stale_reads[:, None, :] * held[None, :, :], axis=2)
    dma = pltpu.SemaphoreType.DMA
    vmem = pltpu.VMEM
    smem_spec = pl.BlockSpec(memory_space=pltpu.SMEM)
    any_spec = pl.BlockSpec(memory_space=pl.ANY)
    copies = 3 + 6 + 3 + HALVES * (4 + 2 + 3 + 3 * BLOCKS) + BLOCKS
    return pl.pallas_call(
        kernel,
        out_shape=jax.ShapeDtypeStruct((rows, columns), BF16),
        in_specs=[smem_spec] * 2 + [any_spec] * 6,
        out_specs=pl.BlockSpec(memory_space=pltpu.VMEM),
        scratch_shapes=[
            vmem((HEADS, tokens, HD), BF16),
            vmem((2, 3, TILE, width), BF16),
            vmem((HEADS, 2, SLOTS * TILE, HD), BF16),
            vmem((SIDE, HEADS, tokens, HD), BF16),
            vmem((SIDE, 4, SLOTS * TILE, HD), BF16),
            vmem((2, keys, HD), BF16),
            vmem((2, keys, 2 * HD), BF16),
            vmem((8, keys), F32),
            vmem((LANES, HD), F32),
            vmem((HALVES, SIDE, HEADS, half, HD), BF16),
            vmem((HALVES, SIDE, 8, LANES), F32),
            vmem((HALVES, 2, HEADS, half, HD), BF16),
            vmem((HALVES, 2, 8, LANES), F32),
            vmem((HALVES, HEADS, half, HD), BF16),
            vmem((HALVES, 8, LANES), F32),
            vmem((HALVES, HEADS, half, HD), BF16),
            vmem((HALVES, 8, LANES), F32),
            vmem((HALVES, HEADS, half, HD), BF16),
            vmem((HALVES, HEADS, half, HD), BF16),
            vmem((depth, columns), BF16),
            vmem((HALVES, BLOCKS, SIDE, rows, cols), BF16),
            vmem((HALVES, BLOCKS, rows, cols), BF16),
            vmem((2, HALVES, BLOCKS, rows, cols), BF16),
            vmem((BLOCKS, rows, cols), BF16),
            vmem((BLOCKS, rows, cols), BF16),
            dma((HEADS * 3 + 3,)),
            dma((copies,)),
            dma((copies,)),
        ],
        compiler_params=pltpu.CompilerParams(
            collective_id=0, has_side_effects=True, vmem_limit_bytes=56 * 2**20
        ),
        name="attend_and_project",
    )(
        refresh,
        wanted,
        queries,
        fresh_key.reshape(3, TILE, width),
        fresh_value.reshape(3, TILE, width),
        stale_key,
        stale_value,
        out_weight,
    )


def solution(mesh):
    return jax.shard_map(
        on_device,
        mesh=mesh,
        in_specs=(
            P(("cfg", "seq"), "head"),
            P(("cfg", "seq"), "head"),
            P(("cfg", "seq"), "head"),
            P(("cfg", "seq"), "head"),
            P(("cfg", "seq"), "head"),
            P("cfg"),
            P("cfg"),
            P("cfg", None),
            P("head", None),
        ),
        out_specs=P(("cfg", "seq", "head"), None),
        check_vma=False,
    )
```

time: 548 us -> 131 us (0.24)
  waiting for transfers between devices: 383 us -> 0 us
  Pallas kernels: 0 us -> 126 us
  matrix products: 66.6 us -> 0 us
  local copies, waits for them, and re-layouts: 34.3 us -> 1.84 us
  other arithmetic: 32.3 us -> 2.37 us
  starting transfers between devices: 15.7 us -> 0 us
  between operations: 13.3 us -> 0.01 us
    all_to_all x2 -> x0, waiting for transfers between devices: 258 us -> none  [the longest x1 133 us: on_device(): lax.all_to_all(send_value, 'seq', split_axis=0, concat_axis=0, tiled=True)]
    pallas_call x0 -> x1, Pallas kernels: none -> 126 us  [on_device(): pl.pallas_call(kernel, out_shape=jax.ShapeDtypeStruct((rows, columns), BF...]
    reduce_scatter x1 -> x0, waiting for transfers between devices: 124 us -> none  [on_device(): lax.psum_scatter(jnp.dot(attended, out_weight, preferred_element_type=jnp...]
    dot_general x7 -> x0, matrix products: 66.6 us -> none  [the longest x2 29.7 us: attend(): jnp.einsum('qhd,khd->qhk', query3, keys3, preferred_element_type=jnp.floa...]
    reduce_sum x6 -> x1, other arithmetic: 32.1 us -> 1.65 us  [on_device(): wanted = jnp.sum(stale_reads[:, None, :] * held[None, :, :], axis=2)]
    all_to_all x2 -> x0, starting transfers between devices: 15.4 us -> none  [the longest x1 8.65 us: on_device(): lax.all_to_all(send_value, 'seq', split_axis=0, concat_axis=0, tiled=True)]
    another operation x2 -> x0, local copies, waits for them, and re-layouts: 10.9 us -> none  [the longest x1 6.98 us: attend(): keys3 = keys.reshape(count, heads_here, HD)]
    all_gather x1 -> x0, local copies, waits for them, and re-layouts: 10.8 us -> none  [on_device(): lax.all_gather(fresh_value, 'seq', axis=0, tiled=True)]
  transfers between devices with their start and end apart: 5 -> 0, of which waited for: 3 -> 0; matrix products, arithmetic and copies ran while one was open for 17% -> 0% of each run, Pallas kernels for 0% -> 0%
where the time goes in v2:
time: 131 us; the launch traced here: 130 us
  Pallas kernels  126 us (96%)
  other arithmetic  2.37 us (2%)
  local copies, waits for them, and re-layouts  1.84 us (1%)
    pallas_call x1, Pallas kernels, on_device(): pl.pallas_call(kernel, out_shape=jax.ShapeDtypeStruct((rows, columns), BF...  126 us

profile of v2, /device:TPU:32, one launch (start us, length us, event | category | flops | bytes accessed | tf_op | source)
XLA Modules:
  0.0 130.4 jit_solution(12948294169449018647)
XLA Ops:
  0.0 0.7 fusion
  0.7 1.6 %multiply_reduce_fusion.wanted = s32[16,48]{1,0:T(8,128)} fusion(s32[48,48]{1,0:T(8,128)S(1)} %fusion, s32[16,48]{1,0:T(8,128)} %param.16), kind=kLoop, calls=%fused_computation | loop fusion | flops 72960 | bytes 15360 | tf_op jit(solution)/shard_map/reduce_sum | solution.py:377
  2.4 126.2 %attend_and_project.1 = bf16[48,5120]{1,0:T(8,128)(2,1)} custom-call(s32[48]{0:T(128)} %refresh.1, s32[16,48]{1,0:T(8,128)} %multiply_reduce_fusion.wanted, bf16[384,640]{1,0:T(8,128)(2,1)} %q_hbm.1, bf16[3,128,640]{2,1,0:T(8,128)(2,1)} %bitcast.2, bf16[3,128,640]{2,1,0:T(8,128)(2,1)} %bitcast.3, bf16[384,640]{1,0:T(8,128)(2,1)} %sk_hbm.1, ...), custom_call_target="tpu_custom_call" | custom-call | tf_op jit(solution)/shard_map/attend_and_project/pallas_call | solution.py:383
  128.6 1.8 %copy.11 = bf16[48,5120]{1,0:T(8,128)(2,1)} copy(bf16[48,5120]{1,0:T(8,128)(2,1)} %attend_and_project.1) | data formatting | bytes 983040

commit v3 on v2

--- a/solution.py
+++ b/solution.py
@@ -15,6 +15,7 @@
 SLOTS = 5
 HALVES = 2
 BLOCKS = 4
+GROUP = 4
 LANES = 256
 MESH = pl.DeviceIdType.MESH
 NEG = -1e30
@@ -150,47 +151,56 @@
             pack[h, kind, TILE : 2 * TILE] = jnp.where(r2 > 0, tile2, tile1)
     for copy in stale_loads:
         copy.wait()
-    row_kv = []
-    for other, device in row:
-        for part, source in enumerate((other, last)):
-            row_kv.append(send(pack.at[source], kv.at[yi, pl.ds(2 * part, 2)], device))
+    row_kv = [
+        [send(pack.at[other], kv.at[yi, pl.ds(0, 2)], device) for other, device in row],
+        [send(pack.at[last], kv.at[yi, pl.ds(2, 2)], device) for _, device in row],
+    ]
     w_load = load(w_hbm, w)
     kv[yi, 0:2] = pack[yi]
     kv[yi, 2:4] = pack[last]
-    values[:, :, HD:] = jnp.ones((2, values.shape[1], HD), BF16)
+    values[:, :, :, HD:] = jnp.ones((2, GROUP, values.shape[2], HD), BF16)
     stats[...] = jnp.zeros(stats.shape, F32)
 
     for copy in row_q:
         copy.wait_recv()
-    q_far = send(qall.at[zi], qall.at[zi], to_z2)
-    q_near = send(qall.at[zi], qall.at[zi], to_z1)
-    q_far.wait_recv()
-    q_relay = send(qall.at[z2], qall.at[z2], to_z1)
-
-    for copy in row_kv:
-        copy.wait_recv()
-    for part in range(2):
+    starts = [pl.multiple_of((1 - zh) * half, half), pl.multiple_of(zh * half, half)]
+
+    def give_q(t, zr, device):
+        part = qall.at[zr, :, pl.ds(starts[t], half)]
+        return send(part, part, device)
+
+    q_far = [give_q(0, zi, to_z2), None]
+    q_near = [give_q(0, zi, to_z1), None]
+    q_far[0].wait_recv()
+    q_relay = [give_q(0, z2, to_z1), None]
+    q_far[1] = give_q(1, zi, to_z2)
+    q_near[1] = give_q(1, zi, to_z1)
+
+    def gather_fresh(part):
+        for copy in row_kv[part]:
+            copy.wait_recv()
         for source in range(SIDE):
             cut = slice(source * 2 * TILE, (source + 1) * 2 * TILE)
-            keys[part, cut] = kv[source, 2 * part, 0 : 2 * TILE]
-            values[part, cut, 0:HD] = kv[source, 2 * part + 1, 0 : 2 * TILE]
+            fresh_keys = kv[source, 2 * part, 0 : 2 * TILE]
+            fresh_values = kv[source, 2 * part + 1, 0 : 2 * TILE]
+            for g in range(GROUP):
+                keys[part, g, cut] = fresh_keys
+                values[part, g, cut, 0:HD] = fresh_values
+
     for source in range(SIDE):
         base = 3 * (zi * SIDE + source)
         filled = refresh[base] + refresh[base + 1] + refresh[base + 2]
         cut = source * 2 * TILE
-        bias[0:1, cut : cut + TILE] = jnp.zeros((1, TILE), F32)
-        bias[0:1, cut + TILE : cut + 2 * TILE] = jnp.full(
-            (1, TILE), jnp.where(filled > 1, 0.0, NEG), F32
-        )
+        for g in range(GROUP):
+            bias[g, 0:1, cut : cut + TILE] = jnp.zeros((1, TILE), F32)
+            bias[g, 0:1, cut + TILE : cut + 2 * TILE] = jnp.full(
+                (1, TILE), jnp.where(filled > 1, 0.0, NEG), F32
+            )
 
     fresh_rows = SIDE * 2 * TILE
 
-    def attend(t, zr, place):
-        start_row = pl.multiple_of(jnp.where(t == 0, 1 - zh, zh) * half, half)
-
-        def item(k, carry):
-            is_last = jnp.where(k == last, 1, 0)
-            reader = zr * SIDE + k * (1 - is_last) + yi * is_last
+    def attend_items(t, part, items):
+        for g, (_, reader, _, _) in enumerate(items):
             for source in range(SIDE):
                 base = 3 * (zi * SIDE + source)
                 flags = [wanted[reader, base + j] for j in range(3)]
@@ -202,28 +212,41 @@
                     ]
                     return jnp.where(flags[1] > 0, tile1, jnp.where(flags[2] > 0, tile2, tile0))
 
-                keys[is_last, cut] = pick(2 * is_last)
-                values[is_last, cut, 0:HD] = pick(2 * is_last + 1)
+                keys[part, g, cut] = pick(2 * part)
+                values[part, g, cut, 0:HD] = pick(2 * part + 1)
                 used = flags[0] + flags[1] + flags[2]
-                bias[0:1, cut] = jnp.full((1, TILE), jnp.where(used > 0, 0.0, NEG), F32)
-            score = lax.dot_general(
-                qall[zr, k, pl.ds(start_row, half)],
-                keys[is_last],
+                bias[g, 0:1, cut] = jnp.full((1, TILE), jnp.where(used > 0, 0.0, NEG), F32)
+        scores = [
+            lax.dot_general(
+                qall[zr, k, pl.ds(starts[t], half)],
+                keys[part, g],
                 (((1,), (1,)), ((), ())),
                 preferred_element_type=F32,
             )
-            score = score * LOG2_SCALE + bias[0:1, :]
+            for g, (zr, _, k, _) in enumerate(items)
+        ]
+        lane = lax.broadcasted_iota(jnp.int32, (half, HD), 1)
+        logs = jnp.zeros((half, HD), F32)
+        for g, (_, _, k, place) in enumerate(items):
+            score = scores[g] * LOG2_SCALE + bias[g, 0:1, :]
             top = jnp.max(score, axis=1, keepdims=True)
             weight = jnp.exp2(score - top).astype(BF16)
-            both = jnp.dot(weight, values[is_last], preferred_element_type=F32)
+            both = jnp.dot(weight, values[part, g], preferred_element_type=F32)
             total = both[:, HD:]
             o_own[t, place, k] = (both[:, :HD] / total).astype(BF16)
-            lane = lax.broadcasted_iota(jnp.int32, (half, HD), 1)
-            stats[0:half] = jnp.where(lane == k, top + jnp.log2(total), stats[0:half])
-            return carry
-
-        lax.fori_loop(0, HEADS, item, 0)
-        l_own[t, place] = stats[...].T[0:8, :]
+            logs = jnp.where(lane == g, top + jnp.log2(total), logs)
+        stats[t, part, 0:half] = logs
+
+    def attend(t, zr, place):
+        attend_items(t, 0, [(zr, zr * SIDE + k, k, place) for k in range(last)])
+        l_own[t, 0, place] = stats[t, 0].T[0:8, :]
+
+    def attend_last(t):
+        places = (zi, z1, z2, z3)
+        attend_items(t, 1, [(zr, zr * SIDE + yi, last, i) for i, zr in enumerate(places)])
+        logs = stats[t, 1].T[0:8, :]
+        for place in range(SIDE):
+            l_own[t, 1, place, last : last + 1] = logs[place : place + 1]
 
     def shares(logs):
         top = functools.reduce(jnp.maximum, logs)
@@ -239,33 +262,44 @@
             mixed += piece.astype(F32) * factors[0:half, 8 * i + k : 8 * i + k + 1]
         return mixed.astype(BF16)
 
-    near_copies = [[], []]
-    far_copies = [[], []]
+    spans = ((0, last), (last, HEADS))
+    near_copies = {}
+    far_copies = {}
     row_copies = [[], []]
 
-    def return_near(t, place, slot):
-        near_copies[t].append(send(o_own.at[t, place], o_near.at[t, slot], to_z1))
-        near_copies[t].append(send(l_own.at[t, place], l_near.at[t, slot], to_z1))
-
-    def merge(t):
-        for copy in near_copies[t]:
+    def return_near(t, part, place, slot):
+        first, stop = spans[part]
+        span = pl.ds(first, stop - first)
+        copies = near_copies.setdefault((t, part), [])
+        copies.append(send(o_own.at[t, place, span], o_near.at[t, slot, span], to_z1))
+        copies.append(send(l_own.at[t, part, place], l_near.at[t, part, slot], to_z1))
+
+    def merge(t, part):
+        first, stop = spans[part]
+        for copy in near_copies[t, part]:
             copy.wait_recv()
-        l_merge[t], factors = shares([l_own[t, 2], l_near[t, 1]])
-        for k in range(HEADS):
+        l_merge[t, part], factors = shares([l_own[t, part, 2], l_near[t, part, 1]])
+        for k in range(first, stop):
             o_merge[t, k] = mix([o_own[t, 2, k], o_near[t, 1, k]], factors, k)
-        far_copies[t].append(send(o_merge.at[t], o_far.at[t], to_z2))
-        far_copies[t].append(send(l_merge.at[t], l_far.at[t], to_z2))
-
-    def combine(t):
-        for copy in far_copies[t]:
+        span = pl.ds(first, stop - first)
+        far_copies[t, part] = [
+            send(o_merge.at[t, span], o_far.at[t, span], to_z2),
+            send(l_merge.at[t, part], l_far.at[t, part], to_z2),
+        ]
+
+    def combine(t, part):
+        first, stop = spans[part]
+        for copy in far_copies[t, part]:
             copy.wait_recv()
-        _, factors = shares([l_own[t, 0], l_near[t, 0], l_far[t]])
-        for k in range(HEADS):
+        _, factors = shares([l_own[t, part, 0], l_near[t, part, 0], l_far[t, part]])
+        for k in range(first, stop):
             comb[t, k] = mix([o_own[t, 0, k], o_near[t, 0, k], o_far[t, k]], factors, k)
-        for other, device in row:
-            row_copies[t].append(send(comb.at[t, other], att5.at[t, yi], device))
-        att5[t, yi] = comb[t, yi]
-        att5[t, last] = comb[t, last]
+        if part == 0:
+            for other, device in row:
+                row_copies[t].append(send(comb.at[t, other], att5.at[t, yi], device))
+            att5[t, yi] = comb[t, yi]
+        else:
+            att5[t, last] = comb[t, last]
 
     part_rows, part_columns = pbuf.shape[3], pbuf.shape[4]
     order = (0, BLOCKS // 2, 1, BLOCKS // 2 + 1)
@@ -296,9 +330,9 @@
             ).astype(BF16)
             for x in range(SIDE):
                 pbuf[t, block, x] = product[x * part_rows : (x + 1) * part_rows]
-            _, far, near, _ = plans[t, block]
-            far.start()
-            near.start()
+            plans[t, block][1].start()
+        for block in order:
+            plans[t, block][2].start()
 
     def relay(t):
         for block in order:
@@ -319,31 +353,47 @@
             + fbuf[1, t, block].astype(F32)
         )
 
+    gather_fresh(0)
     attend(0, zi, 0)
-    q_near.wait_recv()
+    q_near[0].wait_recv()
     attend(0, z1, 1)
-    return_near(0, 1, 0)
-    q_relay.wait_recv()
+    return_near(0, 0, 1, 0)
+    q_relay[0].wait_recv()
     attend(0, z3, 3)
-    return_near(0, 3, 1)
+    return_near(0, 0, 3, 1)
+    q_far[1].wait_recv()
+    q_relay[1] = give_q(1, z2, to_z1)
     attend(0, z2, 2)
+    attend(1, zi, 0)
+    merge(0, 0)
+    q_near[1].wait_recv()
     attend(1, z1, 1)
-    return_near(1, 1, 0)
-    merge(0)
+    return_near(1, 0, 1, 0)
+    gather_fresh(1)
+    attend_last(0)
+    return_near(0, 1, 1, 0)
+    return_near(0, 1, 3, 1)
+    q_relay[1].wait_recv()
     attend(1, z3, 3)
-    return_near(1, 3, 1)
+    return_near(1, 0, 3, 1)
+    merge(0, 1)
+    attend_last(1)
+    return_near(1, 1, 1, 0)
+    return_near(1, 1, 3, 1)
+    combine(0, 0)
     attend(1, z2, 2)
-    combine(0)
-    attend(1, zi, 0)
-    merge(1)
+    combine(0, 1)
+    merge(1, 0)
+    merge(1, 1)
     w_load.wait()
     project(0)
     relay(0)
-    combine(1)
+    combine(1, 0)
+    combine(1, 1)
+    project(1)
     for block in order:
         zsend[block] = reduced(0, block).astype(BF16)
         hi_plans[block].start()
-    project(1)
     relay(1)
     for block in order:
         total = reduced(1, block)
@@ -379,7 +429,7 @@
     vmem = pltpu.VMEM
     smem_spec = pl.BlockSpec(memory_space=pltpu.SMEM)
     any_spec = pl.BlockSpec(memory_space=pl.ANY)
-    copies = 3 + 6 + 3 + HALVES * (4 + 2 + 3 + 3 * BLOCKS) + BLOCKS
+    copies = 3 + 6 + 6 + HALVES * (8 + 4 + 3 + 3 * BLOCKS) + BLOCKS
     return pl.pallas_call(
         kernel,
         out_shape=jax.ShapeDtypeStruct((rows, columns), BF16),
@@ -391,18 +441,18 @@
             vmem((HEADS, 2, SLOTS * TILE, HD), BF16),
             vmem((SIDE, HEADS, tokens, HD), BF16),
             vmem((SIDE, 4, SLOTS * TILE, HD), BF16),
-            vmem((2, keys, HD), BF16),
-            vmem((2, keys, 2 * HD), BF16),
-            vmem((8, keys), F32),
-            vmem((LANES, HD), F32),
+            vmem((2, GROUP, keys, HD), BF16),
+            vmem((2, GROUP, keys, 2 * HD), BF16),
+            vmem((GROUP, 8, keys), F32),
+            vmem((HALVES, 2, LANES, HD), F32),
             vmem((HALVES, SIDE, HEADS, half, HD), BF16),
-            vmem((HALVES, SIDE, 8, LANES), F32),
+            vmem((HALVES, 2, SIDE, 8, LANES), F32),
             vmem((HALVES, 2, HEADS, half, HD), BF16),
+            vmem((HALVES, 2, 2, 8, LANES), F32),
+            vmem((HALVES, HEADS, half, HD), BF16),
             vmem((HALVES, 2, 8, LANES), F32),
             vmem((HALVES, HEADS, half, HD), BF16),
-            vmem((HALVES, 8, LANES), F32),
-            vmem((HALVES, HEADS, half, HD), BF16),
-            vmem((HALVES, 8, LANES), F32),
+            vmem((HALVES, 2, 8, LANES), F32),
             vmem((HALVES, HEADS, half, HD), BF16),
             vmem((HALVES, HEADS, half, HD), BF16),
             vmem((depth, columns), BF16),

time: 131 us -> 124 us (0.947)
  Pallas kernels: 126 us -> 119 us
    pallas_call x1, Pallas kernels: 126 us -> 119 us  [on_device(): pl.pallas_call(kernel, out_shape=jax.ShapeDtypeStruct((rows, columns), BF...]
where the time goes in v3:
time: 124 us; the launch traced here: 123 us
  Pallas kernels  119 us (96%)
  other arithmetic  2.37 us (2%)
  local copies, waits for them, and re-layouts  1.84 us (1%)
    pallas_call x1, Pallas kernels, on_device(): pl.pallas_call(kernel, out_shape=jax.ShapeDtypeStruct((rows, columns), BF...  119 us

profile of v3, /device:TPU:32, one launch (start us, length us, event | category | flops | bytes accessed | tf_op | source)
XLA Modules:
  0.0 123.3 jit_solution(9247028291775853942)
XLA Ops:
  0.0 0.7 fusion
  0.7 1.6 %multiply_reduce_fusion.wanted = s32[16,48]{1,0:T(8,128)} fusion(s32[48,48]{1,0:T(8,128)S(1)} %fusion, s32[16,48]{1,0:T(8,128)} %param.16), kind=kLoop, calls=%fused_computation | loop fusion | flops 72960 | bytes 15360 | tf_op jit(solution)/shard_map/reduce_sum | solution.py:427
  2.4 119.1 %attend_and_project.1 = bf16[48,5120]{1,0:T(8,128)(2,1)} custom-call(s32[48]{0:T(128)} %refresh.1, s32[16,48]{1,0:T(8,128)} %multiply_reduce_fusion.wanted, bf16[384,640]{1,0:T(8,128)(2,1)} %q_hbm.1, bf16[3,128,640]{2,1,0:T(8,128)(2,1)} %bitcast.2, bf16[3,128,640]{2,1,0:T(8,128)(2,1)} %bitcast.3, bf16[384,640]{1,0:T(8,128)(2,1)} %sk_hbm.1, ...), custom_call_target="tpu_custom_call" | custom-call | tf_op jit(solution)/shard_map/attend_and_project/pallas_call | solution.py:433
  121.4 1.8 %copy.11 = bf16[48,5120]{1,0:T(8,128)(2,1)} copy(bf16[48,5120]{1,0:T(8,128)(2,1)} %attend_and_project.1) | data formatting | bytes 983040

commit v4 on v3

--- a/solution.py
+++ b/solution.py
@@ -45,12 +45,16 @@
     stats,
     o_own,
     l_own,
-    o_near,
-    l_near,
-    o_far,
-    l_far,
-    o_merge,
-    l_merge,
+    o_out,
+    l_out,
+    o_mid,
+    l_mid,
+    o_mid_send,
+    l_mid_send,
+    o_back,
+    l_back,
+    o_back_send,
+    l_back_send,
     comb,
     att5,
     w,
@@ -76,8 +80,12 @@
     z1 = zi + 1 - 2 * lax.rem(zi, 2)
     z2 = lax.rem(zi + 2, SIDE)
     z3 = SIDE - 1 - zi
+    inner = jnp.logical_or(zi == 1, zi == 2)
+    outer = jnp.logical_not(inner)
+    zj = jnp.where(inner, z3, z2)
+    zp = jnp.where(inner, z2, z3)
     to_z1 = {"seq": z1 * SIDE + yi}
-    to_z2 = {"seq": z2 * SIDE + yi}
+    to_z3 = {"seq": z3 * SIDE + yi}
     row = []
     for step in (2, 1, 3):
         other = lax.rem(yi + step, SIDE)
@@ -85,10 +93,10 @@
     last = HEADS - 1
     tokens = qpack.shape[1]
     half = tokens // HALVES
-    started = []
+    started = {"all": [], "inner": [], "outer": []}
     count = [0]
 
-    def remote(src, dst, device):
+    def remote(src, dst, device, role="all"):
         index = count[0]
         count[0] += 1
         copy = pltpu.make_async_remote_copy(
@@ -99,11 +107,11 @@
             device_id=device,
             device_id_type=MESH,
         )
-        started.append(copy)
+        started[role].append(copy)
         return copy
 
-    def send(src, dst, device):
-        copy = remote(src, dst, device)
+    def send(src, dst, device, role="all"):
+        copy = remote(src, dst, device, role)
         copy.start()
         return copy
 
@@ -128,7 +136,7 @@
             )
 
     barrier = pltpu.get_barrier_semaphore()
-    peers = [device for _, device in row] + [to_z1, to_z2, to_right, to_left, to_hi]
+    peers = [device for _, device in row] + [to_z1, to_z3, to_right, to_left, to_hi]
     for device in peers:
         pl.semaphore_signal(barrier, inc=1, device_id=device, device_id_type=MESH)
     pl.semaphore_wait(barrier, len(peers))
@@ -165,16 +173,33 @@
         copy.wait_recv()
     starts = [pl.multiple_of((1 - zh) * half, half), pl.multiple_of(zh * half, half)]
 
-    def give_q(t, zr, device):
+    def give_q(t, zr, device, role):
         part = qall.at[zr, :, pl.ds(starts[t], half)]
-        return send(part, part, device)
-
-    q_far = [give_q(0, zi, to_z2), None]
-    q_near = [give_q(0, zi, to_z1), None]
-    q_far[0].wait_recv()
-    q_relay = [give_q(0, z2, to_z1), None]
-    q_far[1] = give_q(1, zi, to_z2)
-    q_near[1] = give_q(1, zi, to_z1)
+        return remote(part, part, device, role)
+
+    q_own = [give_q(t, zi, to_z1, "all") for t in range(HALVES)]
+    q_mid = [give_q(t, zi, to_z3, "inner") for t in range(HALVES)]
+    q_across = [give_q(t, z1, to_z3, "inner") for t in range(HALVES)]
+    q_from_j = [give_q(t, zj, to_z1, "inner") for t in range(HALVES)]
+    q_from_p = [give_q(t, zp, to_z1, "inner") for t in range(HALVES)]
+
+    q_own[0].start()
+
+    @pl.when(inner)
+    def _():
+        q_mid[0].start()
+
+    q_own[0].wait_recv()
+    q_own[1].start()
+
+    @pl.when(inner)
+    def _():
+        q_across[0].start()
+        q_mid[0].wait_recv()
+        q_from_j[0].start()
+        q_mid[1].start()
+        q_across[0].wait_recv()
+        q_from_p[0].start()
 
     def gather_fresh(part):
         for copy in row_kv[part]:
@@ -242,7 +267,7 @@
         l_own[t, 0, place] = stats[t, 0].T[0:8, :]
 
     def attend_last(t):
-        places = (zi, z1, z2, z3)
+        places = (zi, z1, zj, zp)
         attend_items(t, 1, [(zr, zr * SIDE + yi, last, i) for i, zr in enumerate(places)])
         logs = stats[t, 1].T[0:8, :]
         for place in range(SIDE):
@@ -263,37 +288,95 @@
         return mixed.astype(BF16)
 
     spans = ((0, last), (last, HEADS))
-    near_copies = {}
-    far_copies = {}
     row_copies = [[], []]
 
-    def return_near(t, part, place, slot):
-        first, stop = spans[part]
-        span = pl.ds(first, stop - first)
-        copies = near_copies.setdefault((t, part), [])
-        copies.append(send(o_own.at[t, place, span], o_near.at[t, slot, span], to_z1))
-        copies.append(send(l_own.at[t, part, place], l_near.at[t, part, slot], to_z1))
+    def pair(o_src, l_src, o_dst, l_dst, device, role):
+        return [remote(o_src, o_dst, device, role), remote(l_src, l_dst, device, role)]
+
+    out_copies, mid_copies, back_copies = {}, {}, {}
+    for t in range(HALVES):
+        for part, (first, stop) in enumerate(spans):
+            span = pl.ds(first, stop - first)
+            for place in (1, 2, 3):
+                out_copies[t, part, place] = pair(
+                    o_own.at[t, place, span],
+                    l_own.at[t, part, place],
+                    o_out.at[t, place - 1, span],
+                    l_out.at[t, part, place - 1],
+                    to_z1,
+                    "outer",
+                )
+            for i in range(2):
+                mid_copies[t, part, i] = pair(
+                    o_mid_send.at[t, i, span],
+                    l_mid_send.at[t, part, i],
+                    o_mid.at[t, i, span],
+                    l_mid.at[t, part, i],
+                    to_z3,
+                    "inner",
+                )
+            back_copies[t, part] = pair(
+                o_back_send.at[t, span],
+                l_back_send.at[t, part],
+                o_back.at[t, span],
+                l_back.at[t, part],
+                to_z1,
+                "inner",
+            )
+
+    def start(copies):
+        for copy in copies:
+            copy.start()
+
+    def arrive(copies):
+        for copy in copies:
+            copy.wait_recv()
+
+    def give_out(t, part, *places):
+        @pl.when(outer)
+        def _():
+            for place in places:
+                start(out_copies[t, part, place])
 
     def merge(t, part):
-        first, stop = spans[part]
-        for copy in near_copies[t, part]:
-            copy.wait_recv()
-        l_merge[t, part], factors = shares([l_own[t, part, 2], l_near[t, part, 1]])
-        for k in range(first, stop):
-            o_merge[t, k] = mix([o_own[t, 2, k], o_near[t, 1, k]], factors, k)
-        span = pl.ds(first, stop - first)
-        far_copies[t, part] = [
-            send(o_merge.at[t, span], o_far.at[t, span], to_z2),
-            send(l_merge.at[t, part], l_far.at[t, part], to_z2),
-        ]
+        @pl.when(inner)
+        def _():
+            for i, place in ((1, 3), (0, 2)):
+                arrive(out_copies[t, part, place])
+                log, factors = shares([l_own[t, part, place], l_out[t, part, place - 1]])
+                l_mid_send[t, part, i] = log
+                for k in range(*spans[part]):
+                    o_mid_send[t, i, k] = mix(
+                        [o_own[t, place, k], o_out[t, place - 1, k]], factors, k
+                    )
+                start(mid_copies[t, part, i])
+
+    def give_back(t, part):
+        @pl.when(inner)
+        def _():
+            arrive(mid_copies[t, part, 1])
+            log, factors = shares([l_own[t, part, 1], l_mid[t, part, 1]])
+            l_back_send[t, part] = log
+            for k in range(*spans[part]):
+                o_back_send[t, k] = mix([o_own[t, 1, k], o_mid[t, 1, k]], factors, k)
+            start(back_copies[t, part])
 
     def combine(t, part):
-        first, stop = spans[part]
-        for copy in far_copies[t, part]:
-            copy.wait_recv()
-        _, factors = shares([l_own[t, part, 0], l_near[t, part, 0], l_far[t, part]])
-        for k in range(first, stop):
-            comb[t, k] = mix([o_own[t, 0, k], o_near[t, 0, k], o_far[t, k]], factors, k)
+        @pl.when(inner)
+        def _():
+            arrive(out_copies[t, part, 1])
+            arrive(mid_copies[t, part, 0])
+            _, factors = shares([l_own[t, part, 0], l_out[t, part, 0], l_mid[t, part, 0]])
+            for k in range(*spans[part]):
+                comb[t, k] = mix([o_own[t, 0, k], o_out[t, 0, k], o_mid[t, 0, k]], factors, k)
+
+        @pl.when(outer)
+        def _():
+            arrive(back_copies[t, part])
+            _, factors = shares([l_own[t, part, 0], l_back[t, part]])
+            for k in range(*spans[part]):
+                comb[t, k] = mix([o_own[t, 0, k], o_back[t, k]], factors, k)
+
         if part == 0:
             for other, device in row:
                 row_copies[t].append(send(comb.at[t, other], att5.at[t, yi], device))
@@ -355,38 +438,69 @@
 
     gather_fresh(0)
     attend(0, zi, 0)
-    q_near[0].wait_recv()
+
+    @pl.when(outer)
+    def _():
+        q_from_p[0].wait_recv()
+
+    attend(0, zp, 3)
+    give_out(0, 0, 3)
+    q_own[1].wait_recv()
+
+    @pl.when(inner)
+    def _():
+        q_across[1].start()
+        q_mid[1].wait_recv()
+        q_from_j[1].start()
+
+    @pl.when(outer)
+    def _():
+        q_from_j[0].wait_recv()
+
+    attend(0, zj, 2)
+    give_out(0, 0, 2)
+
+    @pl.when(inner)
+    def _():
+        q_across[1].wait_recv()
+        q_from_p[1].start()
+
     attend(0, z1, 1)
-    return_near(0, 0, 1, 0)
-    q_relay[0].wait_recv()
-    attend(0, z3, 3)
-    return_near(0, 0, 3, 1)
-    q_far[1].wait_recv()
-    q_relay[1] = give_q(1, z2, to_z1)
-    attend(0, z2, 2)
+    give_out(0, 0, 1)
     attend(1, zi, 0)
+
+    @pl.when(outer)
+    def _():
+        q_from_j[1].wait_recv()
+
+    attend(1, zj, 2)
+    give_out(1, 0, 2)
     merge(0, 0)
-    q_near[1].wait_recv()
-    attend(1, z1, 1)
-    return_near(1, 0, 1, 0)
     gather_fresh(1)
     attend_last(0)
-    return_near(0, 1, 1, 0)
-    return_near(0, 1, 3, 1)
-    q_relay[1].wait_recv()
-    attend(1, z3, 3)
-    return_near(1, 0, 3, 1)
+    give_out(0, 1, 3, 2, 1)
+
+    @pl.when(outer)
+    def _():
+        q_from_p[1].wait_recv()
+
+    attend(1, zp, 3)
+    give_out(1, 0, 3)
     merge(0, 1)
+    attend(1, z1, 1)
+    give_out(1, 0, 1)
+    give_back(0, 0)
     attend_last(1)
-    return_near(1, 1, 1, 0)
-    return_near(1, 1, 3, 1)
+    give_out(1, 1, 3, 2, 1)
+    give_back(0, 1)
     combine(0, 0)
-    attend(1, z2, 2)
     combine(0, 1)
     merge(1, 0)
     merge(1, 1)
     w_load.wait()
     project(0)
+    give_back(1, 0)
+    give_back(1, 1)
     relay(0)
     combine(1, 0)
     combine(1, 1)
@@ -401,8 +515,18 @@
         out_ref[:, block * part_columns : (block + 1) * part_columns] = (
             total + zrecv[block].astype(F32)
         ).astype(BF16)
-    for copy in started:
+    for copy in started["all"]:
         copy.wait_send()
+
+    @pl.when(inner)
+    def _():
+        for copy in started["inner"]:
+            copy.wait_send()
+
+    @pl.when(outer)
+    def _():
+        for copy in started["outer"]:
+            copy.wait_send()
 
 
 def on_device(
@@ -429,7 +553,7 @@
     vmem = pltpu.VMEM
     smem_spec = pl.BlockSpec(memory_space=pltpu.SMEM)
     any_spec = pl.BlockSpec(memory_space=pl.ANY)
-    copies = 3 + 6 + 6 + HALVES * (8 + 4 + 3 + 3 * BLOCKS) + BLOCKS
+    copies = 3 + 6 + 10 + HALVES * (12 + 8 + 4 + 3 + 3 * BLOCKS) + BLOCKS
     return pl.pallas_call(
         kernel,
         out_shape=jax.ShapeDtypeStruct((rows, columns), BF16),
@@ -447,6 +571,10 @@
             vmem((HALVES, 2, LANES, HD), F32),
             vmem((HALVES, SIDE, HEADS, half, HD), BF16),
             vmem((HALVES, 2, SIDE, 8, LANES), F32),
+            vmem((HALVES, 3, HEADS, half, HD), BF16),
+            vmem((HALVES, 2, 3, 8, LANES), F32),
+            vmem((HALVES, 2, HEADS, half, HD), BF16),
+            vmem((HALVES, 2, 2, 8, LANES), F32),
             vmem((HALVES, 2, HEADS, half, HD), BF16),
             vmem((HALVES, 2, 2, 8, LANES), F32),
             vmem((HALVES, HEADS, half, HD), BF16),

time: 124 us -> 117 us (0.944)
  the two profiles are of different devices: /device:TPU:32 before, /device:TPU:8 now
where the time goes in v4:
time: 117 us
  Pallas kernels  112 us (96%)
  other arithmetic  2.37 us (2%)
  local copies, waits for them, and re-layouts  1.84 us (2%)
    pallas_call x1, Pallas kernels, on_device(): pl.pallas_call(kernel, out_shape=jax.ShapeDtypeStruct((rows, columns), BF...  112 us

profile of v4, /device:TPU:8, one launch (start us, length us, event | category | flops | bytes accessed | tf_op | source)
XLA Modules:
  0.0 116.7 jit_solution(14255095111535967244)
XLA Ops:
  0.0 0.7 fusion
  0.7 1.6 %multiply_reduce_fusion.wanted = s32[16,48]{1,0:T(8,128)} fusion(s32[48,48]{1,0:T(8,128)S(1)} %fusion, s32[16,48]{1,0:T(8,128)} %param.16), kind=kLoop, calls=%fused_computation | loop fusion | flops 72960 | bytes 15360 | tf_op jit(solution)/shard_map/reduce_sum | solution.py:551
  2.4 112.4 %attend_and_project.1 = bf16[48,5120]{1,0:T(8,128)(2,1)} custom-call(s32[48]{0:T(128)} %refresh.1, s32[16,48]{1,0:T(8,128)} %multiply_reduce_fusion.wanted, bf16[384,640]{1,0:T(8,128)(2,1)} %q_hbm.1, bf16[3,128,640]{2,1,0:T(8,128)(2,1)} %bitcast.2, bf16[3,128,640]{2,1,0:T(8,128)(2,1)} %bitcast.3, bf16[384,640]{1,0:T(8,128)(2,1)} %sk_hbm.1, ...), custom_call_target="tpu_custom_call" | custom-call | tf_op jit(solution)/shard_map/attend_and_project/pallas_call | solution.py:557
  114.8 1.8 %copy.11 = bf16[48,5120]{1,0:T(8,128)(2,1)} copy(bf16[48,5120]{1,0:T(8,128)(2,1)} %attend_and_project.1) | data formatting | bytes 983040
